TPU v7x, 32 devices: a whole 2x2x4 slice. The times are simulated.
32 devices in a mesh: grp: 16 (over z, y, x), dir: 2 (over core).
Axes of the slice: x: 2, y: 2, z: 4, core: 2. Of those that a mesh axis runs over, the one named last changes fastest.
Arguments:
- currents_hist: bfloat16 [6, 64, 256], P(None, 'grp'), may hold values from -6 to 6
- spectra_hist: bfloat16 [64, 64, 512], P(None, 'grp', 'dir'), may hold values from -6 to 6
- excitation: float32 [2, 64, 256], P(None, 'grp'), may hold values from -6 to 6
- near_blocks: bfloat16 [64, 8, 6, 256, 256], P('grp', 'dir'), may hold values from -0.0546875 to 0.0546875
- self_inverse: float32 [64, 256, 256], P('grp'), may hold values from -0.375 to 0.375
- aggregate: bfloat16 [64, 256, 512], P('grp', None, 'dir'), may hold values from -0.375 to 0.375
- translate: float32 [64, 512], P(None, 'dir'), may hold values from -1.5 to 1.5
- neighbours: int32 [64, 8], P('grp', 'dir'), may hold values from 0 to 63, as said below
- counts: int32 [64], P('grp'), may hold values from 1 to 8, as said below
- far_sources: int32 [64, 16], P('grp'), may hold values from 0 to 63
- far_classes: int32 [64, 16], P('grp'), may hold values from 0 to 63
- delays: int32 [64], replicated, may hold values from 1 to 64
Outputs:
- currents: bfloat16 [2, 64, 256], P(None, 'grp')
- spectra: bfloat16 [2, 64, 512], P(None, 'grp', 'dir')
Inputs may be any that keep to these rules, and one draw needn't show every extreme that they name: neighbours[g, 0] = g; every neighbour of group g lies among the groups of g's owner, g // 4, or of the owners one before and one after, at 4 groups an owner. `counts`: the first group has all slots live and the last group one.
All inputs are finite; a program needn't handle non-finite values.
Results may differ from a plain program's by a relative error of at most 0.0095.
Values may be sent and summed in bfloat16 or wider, within the bound.
A program may use at most 64 MiB of HBM per device.

v0:
```python
import jax
import jax.numpy as jnp
from jax import lax
from jax.sharding import PartitionSpec as P

STEPS = 2


def with_halo(block, sides, width):
    for axis, dim in sides:
        count = lax.axis_size(axis)
        forward = [(i, i + 1) for i in range(count - 1)]
        backward = [(target, source) for source, target in forward]
        low = lax.ppermute(
            lax.slice_in_dim(block, block.shape[dim] - width, None, axis=dim), axis, forward
        )
        high = lax.ppermute(lax.slice_in_dim(block, 0, width, axis=dim), axis, backward)
        block = jnp.concatenate([low, block, high], axis=dim)
    return block


def full_rim(history, group_dev):
    return with_halo(history, (("grp", 1),), group_dev)


def per_device(
    currents_hist,
    spectra_hist,
    excitation,
    near_blocks,
    self_inverse,
    aggregate,
    translate,
    neighbours,
    counts,
    far_sources,
    far_classes,
    delays,
):
    group_dev = currents_hist.shape[1]
    slots_dev = near_blocks.shape[1]
    window_start = (lax.axis_index("grp") - 1) * group_dev
    slot_ids = lax.axis_index("dir") * slots_dev + jnp.arange(slots_dev, dtype=jnp.int32)
    alive_mask = (slot_ids[None, :] < counts[:, None]).astype(jnp.bfloat16)
    local_ids = neighbours - window_start
    lag_index = delays[far_classes] - 1
    factors = translate[far_classes]
    window = full_rim(currents_hist, group_dev)
    currents_now = currents_hist
    spectra_now = spectra_hist
    gathered = lax.all_gather(spectra_hist, "grp", axis=1, tiled=True)
    out_currents = []
    out_spectra = []
    for iteration in range(STEPS):
        offsets = far_sources - 0
        rows_here = gathered.shape[1]
        inside = (offsets >= 0) & (offsets < rows_here)
        values = gathered[lag_index, jnp.clip(offsets, 0, rows_here - 1), :].astype(jnp.float32)
        incoming = jnp.sum(jnp.where(inside[:, :, None], values * factors, 0.0), axis=1)
        far_part = jnp.einsum(
            "gbd,gd->gb",
            aggregate,
            incoming.astype(jnp.bfloat16),
            preferred_element_type=jnp.float32,
        )
        picked = window[:, local_ids, :] * alive_mask[None, :, :, None]
        partial_value = (
            jnp.einsum("gklrc,lgkc->gr", near_blocks, picked, preferred_element_type=jnp.float32)
            + far_part
        )
        summed = lax.psum(partial_value, "dir")
        remainder = excitation[iteration] - summed
        solved = jnp.einsum("grc,gc->gr", self_inverse, remainder, precision=lax.Precision.HIGHEST)
        stored = solved.astype(jnp.bfloat16)
        spectrum = jnp.einsum(
            "gbd,gb->gd", aggregate, stored, preferred_element_type=jnp.float32
        ).astype(jnp.bfloat16)
        currents_now = jnp.concatenate([stored[None], currents_now[:-1]], axis=0)
        spectra_now = jnp.concatenate([spectrum[None], spectra_now[:-1]], axis=0)
        out_currents.append(stored)
        out_spectra.append(spectrum)
        if iteration + 1 < STEPS:
            window = full_rim(currents_now, group_dev)
            newest_all = lax.all_gather(spectrum[None], "grp", axis=1, tiled=True)
            gathered = jnp.concatenate([newest_all, gathered[:-1]], axis=0)
    return (jnp.stack(out_currents), jnp.stack(out_spectra))


def solution(mesh):
    placed = (
        P(None, "grp", None),
        P(None, "grp", "dir"),
        P(None, "grp", None),
        P("grp", "dir", None, None, None),
        P("grp", None, None),
        P("grp", None, "dir"),
        P(None, "dir"),
        P("grp", "dir"),
        P("grp"),
        P("grp", None),
        P("grp", None),
        P(),
    )
    return jax.shard_map(
        per_device,
        mesh=mesh,
        in_specs=placed,
        out_specs=(P(None, "grp", None), P(None, "grp", "dir")),
        check_vma=False,
    )
```

profile of v0, /device:TPU:0, one launch (start us, length us, event | category | flops | bytes accessed | tf_op | source)
XLA Modules:
  0.0 153.7 jit_solution(16765444413638163782)
XLA Ops:
  7.3 1.6 %copy.27 = bf16[64,4,256]{2,0,1:T(8,128)(2,1)} copy(bf16[64,4,256]{2,1,0:T(4,128)(2,1)} %param.13) | data formatting | bytes 262144 | tf_op args[1]
  8.9 0.7 copy.24
  9.6 4.8 %collective-permute-start = (bf16[6,4,256]{2,0,1:T(8,128)(2,1)S(1)}, bf16[6,4,256]{2,0,1:T(8,128)(2,1)S(1)}, u32[]{:S(2)}, u32[]{:S(2)}) collective-permute-start(bf16[6,4,256]{2,0,1:T(8,128)(2,1)S(1)} %copy.24), channel_id=1, source_target_pairs={{0,2},{2,4},{4,6},{6,8},{8,10},{10,12},{12,14},{14,16},{16,18},{18... | collective-permute-start | bytes 36872 | tf_op jit(solution)/shard_map/ppermute | solution.py:14
  14.5 1.3 collective-permute-start.1
  15.8 0.7 compare_select_fusion.3
  16.6 0.7 compare_select_fusion.2
  17.3 1.4 gather_fusion.1
  19.2 0.7 gather_fusion.3
  20.8 8.0 %fusion.2 = f32[4,1,256,1,1]{2,1,4,3,0:T(1,128)S(1)} fusion(bf16[4,4,6,256,256]{4,3,2,1,0:T(8,128)(2,1)} %param.15, bf16[6,4,4,256,1]{3,0,2,1,4:T(8,128)(2,1)S(1)} %multiply_bitcast_fusion.1), kind=kOutput, calls=%fused_computation.9 | convolution fusion | flops 12582912 | bytes 12636160 | tf_op jit(solution)/shard_map/gklrc,lgkc->gr/dot_general | solution.py:68
  28.8 45.5 %all-gather.4.cloned.1.call-done = bf16[64,64,256]{2,0,1:T(8,128)(2,1)} async-done(((bf16[64,4,256]{2,0,1:T(8,128)(2,1)}), bf16[64,64,256]{2,0,1:T(8,128)(2,1)}) %all-gather.4.cloned.1.call-update) | async-done | bytes 2097168 | tf_op jit(solution)/shard_map/all_gather | solution.py:51
  74.3 2.8 %copy.28 = bf16[64,64,256]{2,1,0:T(8,128)(2,1)S(1)} copy(bf16[64,64,256]{2,0,1:T(8,128)(2,1)} %all-gather.4.cloned.1.call-done) | data formatting | bytes 4194304 | tf_op jit(solution)/shard_map/all_gather | solution.py:51
  77.1 0.8 gather_fusion.2
  78.0 1.3 fusion.16
  79.3 2.5 %psum.14 = f32[4,256]{1,0:T(4,128)S(1)} all-reduce(f32[4,256]{1,0:T(4,128)S(1)} %bitcast_add_fusion.1), channel_id=1, replica_groups=mesh['grp'=16,'dir'=2] {'dir'}, use_global_device_ids=true, to_apply=%region_1.2 | all-reduce | flops 1024 | bytes 8192 | tf_op jit(solution)/shard_map/psum | solution.py:71
  81.8 1.0 fusion.14
  82.8 3.3 %collective-permute-start.2 = (bf16[6,4,256]{2,0,1:T(8,128)(2,1)S(1)}, bf16[6,4,256]{2,0,1:T(8,128)(2,1)S(1)}, u32[]{:S(2)}, u32[]{:S(2)}) collective-permute-start(bf16[6,4,256]{2,0,1:T(8,128)(2,1)S(1)} %pad_maximum_fusion.3), channel_id=1, source_target_pairs={{0,2},{2,4},{4,6},{6,8},{8,10},{10,12},{12,14},{14,16},{16,18},{18... | collective-permute-start | bytes 36872 | tf_op jit(solution)/shard_map/ppermute | solution.py:14
  86.1 1.3 collective-permute-start.3
  87.4 1.4 slice.29
  89.0 39.9 %all-gather.1 = bf16[16,4,256]{2,1,0:T(4,128)(2,1)S(1)} all-gather(bf16[1,4,256]{2,1,0:T(4,128)(2,1)S(1)} %bitcast.106), channel_id=2, replica_groups=mesh['grp'=16,'dir'=2] {'grp'}, dimensions={0}, use_global_device_ids=true | all-gather | bytes 34816 | tf_op jit(solution)/shard_map/all_gather | solution.py:84
  128.9 3.2 %pad_maximum_fusion = bf16[64,64,256]{2,1,0:T(8,128)(2,1)} fusion(bf16[63,64,256]{2,1,0:T(8,128)(2,1)} %slice.29, bf16[1,64,256]{2,1,0:T(8,128)(2,1)S(1)} %reshape.104), kind=kLoop, calls=%fused_computation.6 | loop fusion | flops 1048576 | bytes 4194304 | tf_op jit(solution)/shard_map/concatenate | solution.py:85
  132.0 1.6 %gather_fusion.5 = bf16[64,256]{1,0:T(8,128)(2,1)S(1)} fusion(bf16[64,64,256]{2,1,0:T(8,128)(2,1)} %pad_maximum_fusion, s32[64]{0:T(128)S(1)} %reshape.76), kind=kCustom, calls=%fused_computation.5 | custom fusion | bytes 66048 | tf_op jit(solution)/shard_map/gather | solution.py:58
  134.7 7.9 %fusion = f32[4,1,256,1,1]{2,1,4,3,0:T(1,128)S(1)} fusion(bf16[4,4,6,256,256]{4,3,2,1,0:T(8,128)(2,1)} %param.15, bf16[6,4,4,256,1]{3,0,2,1,4:T(8,128)(2,1)S(1)} %multiply_bitcast_fusion), kind=kOutput, calls=%fused_computation.7 | convolution fusion | flops 12582912 | bytes 12636160 | tf_op jit(solution)/shard_map/gklrc,lgkc->gr/dot_general | solution.py:68
  142.6 2.5 %psum.15 = f32[4,256]{1,0:T(4,128)S(1)} all-reduce(f32[4,256]{1,0:T(4,128)S(1)} %bitcast_add_fusion), channel_id=1, replica_groups=mesh['grp'=16,'dir'=2] {'dir'}, use_global_device_ids=true, to_apply=%region_3.4 | all-reduce | flops 1024 | bytes 8192 | tf_op jit(solution)/shard_map/psum | solution.py:71
  145.1 1.0 fusion.8
  (55 shorter events, 3.7 us)
Async XLA Ops:
  7.2 74.6 %copy-start = (f32[4,256,256]{2,1,0:T(8,128)S(1)}, f32[4,256,256]{2,1,0:T(8,128)}, u32[]{:S(2)}) copy-start(f32[4,256,256]{2,1,0:T(8,128)} %param.16) | copy-start | bytes 3145732
  7.2 11.8 %copy-start.6 = (s32[4]{0:T(128)S(1)}, s32[4]{0:T(128)}, u32[]{:S(2)}) copy-start(s32[4]{0:T(128)} %param.20) | copy-start | bytes 52
  7.2 11.8 %copy-start.5 = (s32[4,16]{1,0:T(4,128)S(1)}, s32[4,16]{1,0:T(4,128)}, u32[]{:S(2)}) copy-start(s32[4,16]{1,0:T(4,128)} %param.21) | copy-start | bytes 772
  7.2 12.0 %copy-start.3 = (f32[64,256]{1,0:T(8,128)S(1)}, f32[64,256]{1,0:T(8,128)}, u32[]{:S(2)}) copy-start(f32[64,256]{1,0:T(8,128)} %param.18) | copy-start | bytes 196612
  7.2 67.1 %all-gather.4.cloned.1.call-start = ((), (), s32[]{:S(2)}) async-start(), calls=%async_computation | async-start | bytes 2228224 | tf_op jit(solution)/shard_map/all_gather | solution.py:51
  9.6 10.2 %collective-permute-start = (bf16[6,4,256]{2,0,1:T(8,128)(2,1)S(1)}, bf16[6,4,256]{2,0,1:T(8,128)(2,1)S(1)}, u32[]{:S(2)}, u32[]{:S(2)}) collective-permute-start(bf16[6,4,256]{2,0,1:T(8,128)(2,1)S(1)} %copy.24), channel_id=1, source_target_pairs={{0,2},{2,4},{4,6},{6,8},{8,10},{10,12},{12,14},{14,16},{16,18},{18... | collective-permute-start | bytes 36872 | tf_op jit(solution)/shard_map/ppermute | solution.py:14
  14.5 5.6 %collective-permute-start.1 = (bf16[6,4,256]{2,0,1:T(8,128)(2,1)S(1)}, bf16[6,4,256]{2,0,1:T(8,128)(2,1)S(1)}, u32[]{:S(2)}, u32[]{:S(2)}) collective-permute-start(bf16[6,4,256]{2,0,1:T(8,128)(2,1)S(1)} %copy.24), channel_id=1, source_target_pairs={{2,0},{4,2},{6,4},{8,6},{10,8},{12,10},{14,12},{16,14},{18,16},{20... | collective-permute-start | bytes 36872 | tf_op jit(solution)/shard_map/ppermute | solution.py:17
  28.8 52.9 %copy-start.4 = (f32[2,4,256]{2,1,0:T(4,128)S(1)}, f32[2,4,256]{2,1,0:T(4,128)}, u32[]{:S(2)}) copy-start(f32[2,4,256]{2,1,0:T(4,128)} %param.14) | copy-start | bytes 24580
  82.7 6.1 %copy-start.1 = (bf16[4,256,256]{2,1,0:T(8,128)(2,1)S(1)}, bf16[4,256,256]{2,1,0:T(8,128)(2,1)}, u32[]{:S(2)}) copy-start(bf16[4,256,256]{2,1,0:T(8,128)(2,1)} %param.17) | copy-start | bytes 1572868
  82.8 51.2 %collective-permute-start.2 = (bf16[6,4,256]{2,0,1:T(8,128)(2,1)S(1)}, bf16[6,4,256]{2,0,1:T(8,128)(2,1)S(1)}, u32[]{:S(2)}, u32[]{:S(2)}) collective-permute-start(bf16[6,4,256]{2,0,1:T(8,128)(2,1)S(1)} %pad_maximum_fusion.3), channel_id=1, source_target_pairs={{0,2},{2,4},{4,6},{6,8},{8,10},{10,12},{12,14},{14,16},{16,18},{18... | collective-permute-start | bytes 36872 | tf_op jit(solution)/shard_map/ppermute | solution.py:14
  86.1 47.9 %collective-permute-start.3 = (bf16[6,4,256]{2,0,1:T(8,128)(2,1)S(1)}, bf16[6,4,256]{2,0,1:T(8,128)(2,1)S(1)}, u32[]{:S(2)}, u32[]{:S(2)}) collective-permute-start(bf16[6,4,256]{2,0,1:T(8,128)(2,1)S(1)} %pad_maximum_fusion.3), channel_id=1, source_target_pairs={{2,0},{4,2},{6,4},{8,6},{10,8},{12,10},{14,12},{16,14},{18,16},{20... | collective-permute-start | bytes 36872 | tf_op jit(solution)/shard_map/ppermute | solution.py:17
  128.9 4.9 %copy-start.2 = (bf16[4,256,256]{2,1,0:T(8,128)(2,1)S(1)}, bf16[4,256,256]{2,1,0:T(8,128)(2,1)}, u32[]{:S(2)}) copy-start(bf16[4,256,256]{2,1,0:T(8,128)(2,1)} %param.17) | copy-start | bytes 1572868
Sparse Core Ops, SparseCore 0:
  10.8 63.4 all-gather.3
where the time goes:
time: 154 us
  waiting for transfers between devices  45.8 us (30%)
  blocking collectives  44.8 us (29%)
  matrix products  19.7 us (13%)
  between operations  14.2 us (9%)
  local copies, waits for them, and re-layouts  12.7 us (8%)
  starting transfers between devices  10.8 us (7%)
  other arithmetic  5.69 us (4%)
    all_gather x1, waiting for transfers between devices, per_device(): gathered = lax.all_gather(spectra_hist, 'grp', axis=1, tiled=True)  45.5 us
    all_gather x1, blocking collectives, per_device(): newest_all = lax.all_gather(spectrum[None], 'grp', axis=1, tiled=True)  39.9 us
    dot_general x2, matrix products, per_device(): jnp.einsum('gklrc,lgkc->gr', near_blocks, picked, preferred_element_type=...  15.9 us
    ppermute x2, starting transfers between devices, with_halo(): lax.ppermute(lax.slice_in_dim(block, block.shape[dim] - width, None, axis...  8.14 us
    psum x2, blocking collectives, per_device(): summed = lax.psum(partial_value, 'dir')  4.93 us
    concatenate x1, other arithmetic, per_device(): gathered = jnp.concatenate([newest_all, gathered[:-1]], axis=0)  3.15 us
  transfers between devices with their start and end apart: 5, of which 2 were waited for; matrix products, arithmetic and copies ran while one was open for 13% of the time, Pallas kernels for 0%

commit v1 on v0

v1 whole, which is shorter than its diff:
```python
import functools

import jax
import jax.numpy as jnp
from jax import lax
from jax.experimental import pallas as pl
from jax.experimental.pallas import tpu as pltpu
from jax.sharding import PartitionSpec as P

STEPS = 2
MESH = pl.DeviceIdType.MESH
F32 = jnp.float32
BF16 = jnp.bfloat16


def mm(a, b, ca=1, cb=0):
    return lax.dot_general(a, b, (((ca,), (cb,)), ((), ())), preferred_element_type=F32)


def parts(x):
    high = x.astype(BF16)
    return high, (x - high.astype(F32)).astype(BF16)


def kernel(
    n,
    nd,
    nbr_s,
    cnt_s,
    hist_v,
    spec_v,
    exc_v,
    src_v,
    cls_v,
    del_v,
    tr_v,
    near_h,
    inv_h,
    agg_h,
    cur_o,
    spec_o,
    near_v,
    inv_v,
    agg_v,
    inv_hi,
    inv_lo,
    codes,
    win,
    cwin,
    nacc,
    out1,
    out2,
    in1,
    in2,
    sums,
    wide,
    near_sem,
    inv_sem,
    agg_sem,
    code_tx,
    code_rx,
    win_tx,
    win_rx,
    cwin_tx,
    cwin_rx,
    p1_tx,
    p1_rx,
    p2_tx,
    p2_rx,
    sum_tx,
    sum_rx,
):
    gd, slots, lags, nb, _ = near_h.shape
    hf, _, dirs = spec_v.shape
    ncls = tr_v.shape[0]
    far = src_v.shape[1]
    packed = in1.shape[2] != dirs
    me = lax.axis_index("grp")
    mine = lax.axis_index("dir")
    following, before = lax.rem(me + 1, n), lax.rem(me + n - 1, n)

    def near_copy(i):
        g, k = i // slots, i % slots
        return pltpu.make_async_copy(near_h.at[g, k], near_v.at[g, k], near_sem.at[i])

    agg_copy = pltpu.make_async_copy(agg_h, agg_v, agg_sem)
    inv_copy = pltpu.make_async_copy(inv_h, inv_v, inv_sem)

    barrier = pltpu.get_barrier_semaphore()

    @pl.loop(1, n)
    def _(off):
        pl.semaphore_signal(barrier, inc=1, device_id={"grp": lax.rem(me + off, n)}, device_id_type=MESH)

    for off in range(1, nd):
        pl.semaphore_signal(barrier, inc=1, device_id={"dir": lax.rem(mine + off, nd)}, device_id_type=MESH)

    inv_copy.start()

    @pl.loop(0, gd * slots)
    def _(i):
        near_copy(i).start()

    agg_copy.start()

    own = src_v[...] * ncls + cls_v[...]
    codes[me] = jnp.full(codes.shape[1:], -1, jnp.int32)
    codes[me, 0:gd, 0:far] = own
    codes[me, gd : 2 * gd, 0:far] = own
    win[pl.ds(gd, gd)] = jnp.zeros((gd,) + win.shape[1:], F32)
    for lag in range(lags):
        row = hist_v[lag].astype(F32)
        for g in range(gd):
            win[gd + g, lag : lag + 1, :] = row[g : g + 1, :]

    pl.semaphore_wait(barrier, n - 1 + nd - 1)

    def send_all(src, dst, tx, rx):
        def copy(peer, slot):
            return pltpu.make_async_remote_copy(
                src_ref=src(peer),
                dst_ref=dst.at[slot],
                send_sem=tx.at[peer],
                recv_sem=rx.at[slot],
                device_id={"grp": peer},
                device_id_type=MESH,
            )

        @pl.loop(1, n)
        def _(off):
            copy(lax.rem(me + off, n), me).start()

        def arrive():
            @pl.loop(1, n)
            def _(off):
                peer = lax.rem(me + off, n)
                copy(peer, peer).wait_recv()

        def sent():
            @pl.loop(1, n)
            def _(off):
                copy(lax.rem(me + off, n), me).wait_send()

        return arrive, sent

    def send_sides(ref, tx, rx):
        def copy(i, peer, start):
            return pltpu.make_async_remote_copy(
                src_ref=ref.at[pl.ds(gd, gd)],
                dst_ref=ref.at[pl.ds(start, gd)],
                send_sem=tx.at[i],
                recv_sem=rx.at[i],
                device_id={"grp": peer},
                device_id_type=MESH,
            )

        both = (copy(0, following, 0), copy(1, before, 2 * gd))
        for c in both:
            c.start()
        return both

    codes_in, codes_out = send_all(lambda peer: codes.at[me], codes, code_tx, code_rx)
    sides = send_sides(win, win_tx, win_rx)

    lag_ids = lax.broadcasted_iota(jnp.int32, (hf, ncls), 0)
    delay = del_v[...]
    pick1 = (lag_ids == delay - 1).astype(F32).T.astype(BF16)
    pick2 = (lag_ids == delay - 2).astype(F32).T.astype(BF16)
    pick = jnp.concatenate([pick1, pick2], axis=0)
    newest = (lax.broadcasted_iota(jnp.int32, (hf, dirs), 0) == 0).astype(BF16)
    factor = tr_v[...]
    fresh = factor * mm(pick1, newest)
    wide[...] = spec_v[...].astype(F32)
    first, second = [], []
    for s in range(gd):
        got = mm(pick, wide[:, s, :].astype(BF16))
        first.append(factor * got[0:ncls])
        second.append(factor * got[ncls : 2 * ncls])
    p1 = parts(jnp.concatenate(first, axis=0))
    p2 = parts(jnp.concatenate(second, axis=0))

    inv_copy.wait()
    for g in range(gd):
        high, low = parts(inv_v[g])
        inv_hi[g] = high
        inv_lo[g] = low

    def pack(x):
        x = x.reshape(n, 2 * gd, dirs)
        if not packed:
            return x
        half = dirs // 2
        rows = lax.broadcasted_iota(jnp.int32, (n, 2 * gd, half), 1)
        return jnp.where(rows < gd, x[:, :, :half], x[:, :, half:])

    def unpack(x):
        if not packed:
            return x
        low = jnp.concatenate([x[0:gd], x[0:gd]], axis=0)
        high = jnp.concatenate([x[gd:], x[gd:]], axis=0)
        return jnp.concatenate([low, high], axis=1)

    codes_in()
    key = codes[...].reshape(n * 2 * gd, codes.shape[2]) - me * (gd * ncls)
    ids = lax.broadcasted_iota(jnp.int32, (n * 2 * gd, gd * ncls), 1)
    weight = jnp.zeros(ids.shape, F32)
    for f in range(far):
        weight += (key[:, f : f + 1] == ids).astype(F32)
    weight = weight.astype(BF16)
    out1[...] = pack(mm(weight, p1[0]) + mm(weight, p1[1]))
    in1[me] = out1[me]
    p1_in, p1_out = send_all(lambda peer: out1.at[peer], in1, p1_tx, p1_rx)
    older = mm(weight, p2[0]) + mm(weight, p2[1])

    for c in sides:
        c.wait_recv()

    @pl.loop(0, gd)
    def _(g):
        acc = [jnp.zeros((8, nb), F32)] * lags
        for k in range(slots):
            near_copy(g * slots + k).wait()
            local = jnp.clip(nbr_s[g, k] - (me - 1) * gd, 0, 3 * gd - 1)
            alive = (mine * slots + k < cnt_s[g]).astype(F32)
            row = (win[local] * alive).astype(BF16)
            for lag in range(lags):
                acc[lag] += mm(row, near_v[g, k, lag], 1, 1)
        now = acc[0][0:1]
        later = jnp.zeros((1, nb), F32)
        for lag in range(1, lags):
            now += acc[lag][lag : lag + 1]
            later += acc[lag][lag - 1 : lag]
        nacc[g, 0:1, :] = now
        nacc[g, 1:2, :] = later

    agg_copy.wait()

    def solve(step, near, incoming):
        inc = incoming.astype(BF16)
        rows = [near[g] + mm(inc, agg_v[g], 1, 1)[g : g + 1] for g in range(gd)]
        sums[step, mine] = jnp.concatenate(rows, axis=0)

        def copy(peer, slot):
            return pltpu.make_async_remote_copy(
                src_ref=sums.at[step, mine],
                dst_ref=sums.at[step, slot],
                send_sem=sum_tx.at[step, peer],
                recv_sem=sum_rx.at[step, slot],
                device_id={"dir": peer},
                device_id_type=MESH,
            )

        for off in range(1, nd):
            copy(lax.rem(mine + off, nd), mine).start()
        for off in range(1, nd):
            peer = lax.rem(mine + off, nd)
            copy(peer, peer).wait_recv()
        total = sums[step, 0]
        for d in range(1, nd):
            total += sums[step, d]
        rest = exc_v[step] - total
        rest = jnp.concatenate([rest, rest], axis=0)
        high, low = parts(rest)
        both = jnp.concatenate([high, low], axis=0)
        rows = []
        for g in range(gd):
            a = mm(both, inv_hi[g], 1, 1)
            b = mm(high, inv_lo[g], 1, 1)
            rows.append(a[g : g + 1] + a[2 * gd + g : 2 * gd + g + 1] + b[g : g + 1])
        for off in range(1, nd):
            copy(lax.rem(mine + off, nd), mine).wait_send()
        stored = jnp.concatenate(rows, axis=0).astype(BF16)
        cur_o[step] = stored
        return stored

    def radiate(step, stored):
        twice = jnp.concatenate([stored.astype(F32)] * 2, axis=0).astype(BF16)
        rows = [mm(twice, agg_v[g])[g : g + 1] for g in range(gd)]
        spectrum = jnp.concatenate(rows, axis=0).astype(BF16)
        spec_o[step] = spectrum
        return spectrum

    p1_in()
    stored = solve(0, [nacc[g, 0:1, :] for g in range(gd)], unpack(jnp.sum(in1[...], axis=0)))
    wider = stored.astype(F32)
    for g in range(gd):
        cwin[gd + g] = wider[g : g + 1]
    cur_sides = send_sides(cwin, cwin_tx, cwin_rx)
    spectrum = radiate(0, stored).astype(F32)
    q = parts(jnp.concatenate([fresh * spectrum[s : s + 1] for s in range(gd)], axis=0))
    out2[...] = pack(older + mm(weight, q[0]) + mm(weight, q[1]))
    in2[me] = out2[me]
    p2_in, p2_out = send_all(lambda peer: out2.at[peer], in2, p2_tx, p2_rx)
    for c in cur_sides:
        c.wait_recv()
    near = []
    for g in range(gd):
        total = nacc[g, 1:2, :]
        for k in range(slots):
            local = jnp.clip(nbr_s[g, k] - (me - 1) * gd, 0, 3 * gd - 1)
            alive = (mine * slots + k < cnt_s[g]).astype(F32)
            row = (cwin[local] * alive).astype(BF16)
            total += mm(row, near_v[g, k, 0], 1, 1)
        near.append(total)
    p2_in()
    stored = solve(1, near, unpack(jnp.sum(in2[...], axis=0)))
    radiate(1, stored)
    for c in sides:
        c.wait_send()
    for c in cur_sides:
        c.wait_send()
    codes_out()
    p1_out()
    p2_out()


def per_device(
    currents_hist,
    spectra_hist,
    excitation,
    near_blocks,
    self_inverse,
    aggregate,
    translate,
    neighbours,
    counts,
    far_sources,
    far_classes,
    delays,
):
    n, nd = lax.axis_size("grp"), lax.axis_size("dir")
    gd, slots, lags, nb, _ = near_blocks.shape
    hf, _, dirs = spectra_hist.shape
    lane = dirs // 2 if dirs % 256 == 0 else dirs
    vmem = pl.BlockSpec(memory_space=pltpu.VMEM)
    smem = pl.BlockSpec(memory_space=pltpu.SMEM)
    anywhere = pl.BlockSpec(memory_space=pl.ANY)
    dma = pltpu.SemaphoreType.DMA
    return pl.pallas_call(
        functools.partial(kernel, n, nd),
        out_shape=(
            jax.ShapeDtypeStruct((STEPS, gd, nb), BF16),
            jax.ShapeDtypeStruct((STEPS, gd, dirs), BF16),
        ),
        in_specs=[smem] * 2 + [vmem] * 7 + [anywhere] * 3,
        out_specs=(vmem, vmem),
        scratch_shapes=[
            pltpu.VMEM(near_blocks.shape, BF16),
            pltpu.VMEM(self_inverse.shape, F32),
            pltpu.VMEM(aggregate.shape, BF16),
            pltpu.VMEM(self_inverse.shape, BF16),
            pltpu.VMEM(self_inverse.shape, BF16),
            pltpu.VMEM((n, 2 * gd, 128), jnp.int32),
            pltpu.VMEM((3 * gd, 8, nb), F32),
            pltpu.VMEM((3 * gd, 1, nb), F32),
            pltpu.VMEM((gd, 8, nb), F32),
            pltpu.VMEM((n, 2 * gd, lane), F32),
            pltpu.VMEM((n, 2 * gd, lane), F32),
            pltpu.VMEM((n, 2 * gd, lane), F32),
            pltpu.VMEM((n, 2 * gd, lane), F32),
            pltpu.VMEM((STEPS, nd, gd, nb), F32),
            pltpu.VMEM((hf, gd, dirs), F32),
            dma((gd * slots,)),
            dma,
            dma,
            dma((n,)),
            dma((n,)),
            dma((2,)),
            dma((2,)),
            dma((2,)),
            dma((2,)),
            dma((n,)),
            dma((n,)),
            dma((n,)),
            dma((n,)),
            dma((STEPS, nd)),
            dma((STEPS, nd)),
        ],
        compiler_params=pltpu.CompilerParams(
            collective_id=0, has_side_effects=True, vmem_limit_bytes=48 * 1024 * 1024
        ),
        name="march",
    )(
        neighbours,
        counts,
        currents_hist,
        spectra_hist,
        excitation,
        far_sources,
        far_classes,
        delays.reshape(1, -1),
        translate,
        near_blocks,
        self_inverse,
        aggregate,
    )


def solution(mesh):
    placed = (
        P(None, "grp", None),
        P(None, "grp", "dir"),
        P(None, "grp", None),
        P("grp", "dir", None, None, None),
        P("grp", None, None),
        P("grp", None, "dir"),
        P(None, "dir"),
        P("grp", "dir"),
        P("grp"),
        P("grp", None),
        P("grp", None),
        P(),
    )
    return jax.shard_map(
        per_device,
        mesh=mesh,
        in_specs=placed,
        out_specs=(P(None, "grp", None), P(None, "grp", "dir")),
        check_vma=False,
    )
```

time: 154 us -> 38 us (0.25)
  waiting for transfers between devices: 45.8 us -> 0 us
  blocking collectives: 44.8 us -> 0 us
  Pallas kernels: 0 us -> 26.9 us
  matrix products: 19.7 us -> 0 us
  between operations: 14.2 us -> 0.66 us
  starting transfers between devices: 10.8 us -> 0 us
  other arithmetic: 5.69 us -> 0 us
  local copies, waits for them, and re-layouts: 12.7 us -> 9.94 us
    all_gather x1 -> x0, waiting for transfers between devices: 45.5 us -> none  [per_device(): gathered = lax.all_gather(spectra_hist, 'grp', axis=1, tiled=True)]
    all_gather x1 -> x0, blocking collectives: 39.9 us -> none  [per_device(): newest_all = lax.all_gather(spectrum[None], 'grp', axis=1, tiled=True)]
    pallas_call x0 -> x1, Pallas kernels: none -> 26.9 us  [per_device(): pl.pallas_call(functools.partial(kernel, n, nd), out_shape=(jax.ShapeDtyp...]
    dot_general x8 -> x0, matrix products: 19.7 us -> none  [the longest x2 15.9 us: per_device(): jnp.einsum('gklrc,lgkc->gr', near_blocks, picked, preferred_element_type=...]
    ppermute x4 -> x0, starting transfers between devices: 10.7 us -> none  [the longest x2 8.14 us: with_halo(): lax.ppermute(lax.slice_in_dim(block, block.shape[dim] - width, None, axis...]
    unnamed x16 -> x24, local copies, waits for them, and re-layouts: 2.39 us -> 9.94 us
    gather x6 -> x0, local copies, waits for them, and re-layouts: 5.68 us -> none  [the longest x2 2.48 us: per_device(): gathered[lag_index, jnp.clip(offsets, 0, rows_here - 1), :]]
    psum x2 -> x0, blocking collectives: 4.93 us -> none  [per_device(): summed = lax.psum(partial_value, 'dir')]
  transfers between devices with their start and end apart: 5 -> 0, of which waited for: 2 -> 0; matrix products, arithmetic and copies ran while one was open for 13% -> 0% of each run, Pallas kernels for 0% -> 0%
where the time goes in v1:
time: 38 us; the launch traced here: 37.5 us
  Pallas kernels  26.9 us (71%)
  local copies, waits for them, and re-layouts  9.94 us (26%)
  between operations  0.66 us (2%)
    pallas_call x1, Pallas kernels, per_device(): pl.pallas_call(functools.partial(kernel, n, nd), out_shape=(jax.ShapeDtyp...  26.9 us
    unnamed x24, local copies, waits for them, and re-layouts  9.94 us

profile of v1, /device:TPU:0, one launch (start us, length us, event | category | flops | bytes accessed | tf_op | source)
XLA Modules:
  0.0 37.5 jit_solution(16367407884681632466)
XLA Ops:
  0.6 0.0 copy-start
  0.6 1.2 %copy-done = f32[4,256,256]{2,1,0:T(8,128)S(1)} copy-done((f32[4,256,256]{2,1,0:T(8,128)S(1)}, f32[4,256,256]{2,1,0:T(8,128)}, u32[]{:S(2)}) %copy-start) | copy-done | bytes 1048600
  1.9 0.0 copy-start.1
  1.9 1.0 %copy-done.1 = bf16[4,256,256]{2,1,0:T(8,128)(2,1)S(1)} copy-done((bf16[4,256,256]{2,1,0:T(8,128)(2,1)S(1)}, bf16[4,256,256]{2,1,0:T(8,128)(2,1)}, u32[]{:S(2)}) %copy-start.1) | copy-done | bytes 524312
  2.9 0.0 copy-start.2
  2.9 0.9 %copy-done.2 = bf16[64,4,256]{2,1,0:T(4,128)(2,1)S(1)} copy-done((bf16[64,4,256]{2,1,0:T(4,128)(2,1)S(1)}, bf16[64,4,256]{2,1,0:T(4,128)(2,1)}, u32[]{:S(2)}) %copy-start.2) | copy-done | bytes 131096
  3.8 0.0 copy-start.3
  3.8 0.8 %copy-done.3 = f32[64,256]{1,0:T(8,128)S(1)} copy-done((f32[64,256]{1,0:T(8,128)S(1)}, f32[64,256]{1,0:T(8,128)}, u32[]{:S(2)}) %copy-start.3) | copy-done | bytes 65560
  4.6 0.0 copy-start.4
  4.6 0.7 %copy-done.4 = bf16[6,4,256]{2,1,0:T(4,128)(2,1)S(1)} copy-done((bf16[6,4,256]{2,1,0:T(4,128)(2,1)S(1)}, bf16[6,4,256]{2,1,0:T(4,128)(2,1)}, u32[]{:S(2)}) %copy-start.4) | copy-done | bytes 12312
  5.4 0.0 copy-start.5
  5.4 0.7 %copy-done.5 = f32[2,4,256]{2,1,0:T(4,128)S(1)} copy-done((f32[2,4,256]{2,1,0:T(4,128)S(1)}, f32[2,4,256]{2,1,0:T(4,128)}, u32[]{:S(2)}) %copy-start.5) | copy-done | bytes 8216
  6.1 0.0 copy-start.6
  6.1 0.7 %copy-done.6 = s32[4,4]{1,0:T(4,128)S(1)} copy-done((s32[4,4]{1,0:T(4,128)S(1)}, s32[4,4]{1,0:T(4,128)}, u32[]{:S(2)}) %copy-start.6) | copy-done | bytes 88
  6.7 0.0 copy-start.7
  6.7 0.7 %copy-done.7 = s32[4,16]{1,0:T(4,128)S(1)} copy-done((s32[4,16]{1,0:T(4,128)S(1)}, s32[4,16]{1,0:T(4,128)}, u32[]{:S(2)}) %copy-start.7) | copy-done | bytes 280
  7.4 0.0 copy-start.8
  7.4 0.7 %copy-done.8 = s32[4,16]{1,0:T(4,128)S(1)} copy-done((s32[4,16]{1,0:T(4,128)S(1)}, s32[4,16]{1,0:T(4,128)}, u32[]{:S(2)}) %copy-start.8) | copy-done | bytes 280
  8.1 0.0 copy-start.9
  8.1 0.7 %copy-done.9 = s32[4]{0:T(128)S(1)} copy-done((s32[4]{0:T(128)S(1)}, s32[4]{0:T(128)}, u32[]{:S(2)}) %copy-start.9) | copy-done | bytes 40
  8.8 0.7 %copy-done.10 = s32[64]{0:T(128)S(1)} copy-done((s32[64]{0:T(128)S(1)}, s32[64]{0:T(128)}, u32[]{:S(2)}) %copy-start.10) | copy-done | bytes 280
  9.4 26.9 %march.1 = (bf16[2,4,256]{2,1,0:T(4,128)(2,1)S(1)}, bf16[2,4,256]{2,1,0:T(4,128)(2,1)S(1)}) custom-call(s32[4,4]{1,0:T(4,128)S(1)} %copy-done.6, s32[4]{0:T(128)S(1)} %copy-done.9, bf16[6,4,256]{2,1,0:T(4,128)(2,1)S(1)} %copy-done.4, bf16[64,4,256]{2,1,0:T(4,128)(2,1)S(1)} %copy-done.2, f32[2,4,256]{2,1,0:T(4,128)S(1)} %copy-done.5, s32[4,16]{1,0:T(4,128)S(1)} %copy-done.7, ...), custom_call_target="tpu_custom_call" | custom-call | tf_op jit(solution)/shard_map/march/pallas_call | solution.py:339
  36.4 0.6 %copy.16 = bf16[2,4,256]{2,1,0:T(4,128)(2,1)} copy(bf16[2,4,256]{2,1,0:T(4,128)(2,1)S(1)} %get-tuple-element.4) | data formatting | bytes 8192
  36.9 0.6 %copy.17 = bf16[2,4,256]{2,1,0:T(4,128)(2,1)} copy(bf16[2,4,256]{2,1,0:T(4,128)(2,1)S(1)} %get-tuple-element.5) | data formatting | bytes 8192
  (1 shorter events, 0.0 us)
Async XLA Ops:
  0.6 1.2 %copy-start = (f32[4,256,256]{2,1,0:T(8,128)S(1)}, f32[4,256,256]{2,1,0:T(8,128)}, u32[]{:S(2)}) copy-start(f32[4,256,256]{2,1,0:T(8,128)} %inv_h.1) | copy-start | bytes 3145732
  1.9 1.0 %copy-start.1 = (bf16[4,256,256]{2,1,0:T(8,128)(2,1)S(1)}, bf16[4,256,256]{2,1,0:T(8,128)(2,1)}, u32[]{:S(2)}) copy-start(bf16[4,256,256]{2,1,0:T(8,128)(2,1)} %agg_h.1) | copy-start | bytes 1572868
  2.9 0.9 %copy-start.2 = (bf16[64,4,256]{2,1,0:T(4,128)(2,1)S(1)}, bf16[64,4,256]{2,1,0:T(4,128)(2,1)}, u32[]{:S(2)}) copy-start(bf16[64,4,256]{2,1,0:T(4,128)(2,1)} %spec_v.1) | copy-start | bytes 393220
  3.8 0.8 %copy-start.3 = (f32[64,256]{1,0:T(8,128)S(1)}, f32[64,256]{1,0:T(8,128)}, u32[]{:S(2)}) copy-start(f32[64,256]{1,0:T(8,128)} %tr_v.1) | copy-start | bytes 196612
  4.6 0.7 %copy-start.4 = (bf16[6,4,256]{2,1,0:T(4,128)(2,1)S(1)}, bf16[6,4,256]{2,1,0:T(4,128)(2,1)}, u32[]{:S(2)}) copy-start(bf16[6,4,256]{2,1,0:T(4,128)(2,1)} %hist_v.1) | copy-start | bytes 36868
  5.4 0.7 %copy-start.5 = (f32[2,4,256]{2,1,0:T(4,128)S(1)}, f32[2,4,256]{2,1,0:T(4,128)}, u32[]{:S(2)}) copy-start(f32[2,4,256]{2,1,0:T(4,128)} %exc_v.1) | copy-start | bytes 24580
  6.1 0.7 %copy-start.6 = (s32[4,4]{1,0:T(4,128)S(1)}, s32[4,4]{1,0:T(4,128)}, u32[]{:S(2)}) copy-start(s32[4,4]{1,0:T(4,128)} %nbr_s.1) | copy-start | bytes 196
  6.7 0.7 %copy-start.7 = (s32[4,16]{1,0:T(4,128)S(1)}, s32[4,16]{1,0:T(4,128)}, u32[]{:S(2)}) copy-start(s32[4,16]{1,0:T(4,128)} %src_v.1) | copy-start | bytes 772
  7.4 0.7 %copy-start.8 = (s32[4,16]{1,0:T(4,128)S(1)}, s32[4,16]{1,0:T(4,128)}, u32[]{:S(2)}) copy-start(s32[4,16]{1,0:T(4,128)} %cls_v.1) | copy-start | bytes 772
  8.1 0.7 %copy-start.9 = (s32[4]{0:T(128)S(1)}, s32[4]{0:T(128)}, u32[]{:S(2)}) copy-start(s32[4]{0:T(128)} %cnt_s.1) | copy-start | bytes 52
  8.8 0.7 %copy-start.10 = (s32[64]{0:T(128)S(1)}, s32[64]{0:T(128)}, u32[]{:S(2)}) copy-start(s32[64]{0:T(128)} %param.23) | copy-start | bytes 772

commit v2 on v1

--- a/solution.py
+++ b/solution.py
@@ -25,6 +25,20 @@
 def kernel(
     n,
     nd,
+    nbr_h,
+    cnt_h,
+    hist_h,
+    spec_h,
+    exc_h,
+    src_h,
+    cls_h,
+    del_h,
+    tr_h,
+    near_h,
+    inv_h,
+    agg_h,
+    cur_o,
+    spec_o,
     nbr_s,
     cnt_s,
     hist_v,
@@ -34,11 +48,7 @@
     cls_v,
     del_v,
     tr_v,
-    near_h,
-    inv_h,
-    agg_h,
-    cur_o,
-    spec_o,
+    small_sem,
     near_v,
     inv_v,
     agg_v,
@@ -83,9 +93,25 @@
         g, k = i // slots, i % slots
         return pltpu.make_async_copy(near_h.at[g, k], near_v.at[g, k], near_sem.at[i])
 
+    smalls = (
+        (src_h, src_v),
+        (cls_h, cls_v),
+        (hist_h, hist_v),
+        (del_h, del_v),
+        (spec_h, spec_v),
+        (tr_h, tr_v),
+        (nbr_h, nbr_s),
+        (cnt_h, cnt_s),
+        (exc_h, exc_v),
+    )
+    small_copies = [
+        pltpu.make_async_copy(src, dst, small_sem.at[i]) for i, (src, dst) in enumerate(smalls)
+    ]
     agg_copy = pltpu.make_async_copy(agg_h, agg_v, agg_sem)
     inv_copy = pltpu.make_async_copy(inv_h, inv_v, inv_sem)
 
+    for c in small_copies:
+        c.start()
     barrier = pltpu.get_barrier_semaphore()
 
     @pl.loop(1, n)
@@ -103,6 +129,8 @@
 
     agg_copy.start()
 
+    for c in small_copies:
+        c.wait()
     own = src_v[...] * ncls + cls_v[...]
     codes[me] = jnp.full(codes.shape[1:], -1, jnp.int32)
     codes[me, 0:gd, 0:far] = own
@@ -333,8 +361,7 @@
     hf, _, dirs = spectra_hist.shape
     lane = dirs // 2 if dirs % 256 == 0 else dirs
     vmem = pl.BlockSpec(memory_space=pltpu.VMEM)
-    smem = pl.BlockSpec(memory_space=pltpu.SMEM)
-    anywhere = pl.BlockSpec(memory_space=pl.ANY)
+    anywhere = pl.BlockSpec(memory_space=pltpu.HBM)
     dma = pltpu.SemaphoreType.DMA
     return pl.pallas_call(
         functools.partial(kernel, n, nd),
@@ -342,9 +369,19 @@
             jax.ShapeDtypeStruct((STEPS, gd, nb), BF16),
             jax.ShapeDtypeStruct((STEPS, gd, dirs), BF16),
         ),
-        in_specs=[smem] * 2 + [vmem] * 7 + [anywhere] * 3,
+        in_specs=[anywhere] * 12,
         out_specs=(vmem, vmem),
         scratch_shapes=[
+            pltpu.SMEM(neighbours.shape, jnp.int32),
+            pltpu.SMEM(counts.shape, jnp.int32),
+            pltpu.VMEM(currents_hist.shape, BF16),
+            pltpu.VMEM(spectra_hist.shape, BF16),
+            pltpu.VMEM(excitation.shape, F32),
+            pltpu.VMEM(far_sources.shape, jnp.int32),
+            pltpu.VMEM(far_classes.shape, jnp.int32),
+            pltpu.VMEM((1,) + delays.shape, jnp.int32),
+            pltpu.VMEM(translate.shape, F32),
+            dma((9,)),
             pltpu.VMEM(near_blocks.shape, BF16),
             pltpu.VMEM(self_inverse.shape, F32),
             pltpu.VMEM(aggregate.shape, BF16),
@@ -377,7 +414,7 @@
             dma((STEPS, nd)),
         ],
         compiler_params=pltpu.CompilerParams(
-            collective_id=0, has_side_effects=True, vmem_limit_bytes=48 * 1024 * 1024
+            collective_id=0, has_side_effects=True, vmem_limit_bytes=62 * 1024 * 1024
         ),
         name="march",
     )(

time: 38 us -> 30.5 us (0.80)
  local copies, waits for them, and re-layouts: 9.94 us -> 2.53 us
    unnamed x24 -> x2, local copies, waits for them, and re-layouts: 9.94 us -> 2.53 us
where the time goes in v2:
time: 30.5 us; the launch traced here: 30.2 us
  Pallas kernels  27.1 us (89%)
  local copies, waits for them, and re-layouts  2.53 us (8%)
  between operations  0.64 us (2%)
    pallas_call x1, Pallas kernels, per_device(): pl.pallas_call(functools.partial(kernel, n, nd), out_shape=(jax.ShapeDtyp...  27.1 us
    unnamed x2, local copies, waits for them, and re-layouts  2.53 us

profile of v2, /device:TPU:0, one launch (start us, length us, event | category | flops | bytes accessed | tf_op | source)
XLA Modules:
  0.0 30.2 jit_solution(4289487643898076933)
XLA Ops:
  0.6 27.1 %march.1 = (bf16[2,4,256]{2,1,0:T(4,128)(2,1)}, bf16[2,4,256]{2,1,0:T(4,128)(2,1)}) custom-call(s32[4,4]{1,0:T(4,128)} %nbr_h.1, s32[4]{0:T(128)} %cnt_h.1, bf16[6,4,256]{2,1,0:T(4,128)(2,1)} %hist_h.1, bf16[64,4,256]{2,1,0:T(4,128)(2,1)} %spec_h.1, f32[2,4,256]{2,1,0:T(4,128)} %exc_h.1, s32[4,16]{1,0:T(4,128)} %src_h.1, s32[4,16]{1,0:T(4,128)} %cls_h.1, ...), custom_call_target="tpu_custom_call" | custom-call | tf_op jit(solution)/shard_map/march/pallas_call | solution.py:366
  27.7 1.3 %copy.16 = bf16[2,4,256]{2,1,0:T(4,128)(2,1)} copy(bf16[2,4,256]{2,1,0:T(4,128)(2,1)} %get-tuple-element.4) | data formatting | bytes 8192
  29.0 1.3 %copy.17 = bf16[2,4,256]{2,1,0:T(4,128)(2,1)} copy(bf16[2,4,256]{2,1,0:T(4,128)(2,1)} %get-tuple-element.5) | data formatting | bytes 8192
